TPU v7x, 512 devices: a whole 4x8x8 slice. The times are simulated.
512 devices in a mesh: chan: 16 (over x, z_lo), win: 32 (over y, z_hi, core).
Axes of the slice: x: 4, y: 8, z: 8 (z_hi: 2, z_lo: 4; z = z_hi * 4 + z_lo), core: 2. Of those that a mesh axis runs over, the one named last changes fastest.
Arguments:
- spectra: bfloat16 [128, 512, 2, 1024], P('chan', 'win'), may hold values from -27 to 27, as said below
- pair_bin: int32 [128, 3, 8], P('chan'), may hold values from 0 to 127, as said below
- bin_owner: int32 [128], replicated, may hold values from 0 to 31, as said below
Outputs:
- owned: float32 [16, 224, 2, 1024], P('chan', 'win')
Inputs may be any that keep to these rules, and one draw needn't show every extreme that they name: `spectra`: spectra are finite. `pair_bin`: every offset bin of 0 to 127 may occur. `bin_owner`: each index of win owns between 1 and 7 of the 128 bins, and at least one owns exactly 7.
All inputs are finite; a program needn't handle non-finite values.
Results may differ from a plain program's by a relative error of at most 0.0013.
Values may be sent and summed in bfloat16 or wider, within the bound.
A program may use at most 128 MiB of HBM per device.

v0:
```python
import math

import jax
import jax.numpy as jnp
from jax import lax
from jax.sharding import PartitionSpec as P

REACH = 2
BINS_OWN = 4
CAP = 7


def shifted(shard, axis, by):
    size = lax.axis_size(axis)
    return lax.ppermute(shard, axis, [(i, (i + by) % size) for i in range(size)])


def whiten(block_spectra):
    values = block_spectra.astype(jnp.float32)
    power = jnp.mean(values * values, axis=(2, 3), keepdims=True)
    return (values * lax.rsqrt(power + 1e-06)).astype(jnp.bfloat16)


def cross_bins(near_block, far_block, pair_map, bin_count):
    channels = near_block.shape[0]
    rotated = jnp.stack([-far_block[:, :, 1], far_block[:, :, 0]], axis=2)
    partner = jnp.stack([far_block, rotated], axis=3)
    products = jnp.einsum(
        "awcf,bwcjf->abjf", near_block, partner, preferred_element_type=jnp.float32
    )
    rows_flat = products.reshape(channels * channels, products.shape[2] * products.shape[3])
    bin_ids = jnp.arange(bin_count, dtype=jnp.int32)
    selector = (pair_map.reshape(-1)[None, :] == bin_ids[:, None]).astype(jnp.float32)
    binned = jnp.dot(
        selector, rows_flat, precision=lax.Precision.HIGHEST, preferred_element_type=jnp.float32
    )
    return binned.reshape(bin_count, products.shape[2], products.shape[3])


def bin_slots(bin_owner, capacity):
    bin_count = bin_owner.shape[0]
    ranking = jnp.arange(bin_count, dtype=jnp.int32)
    shared_owner = bin_owner[None, :] == bin_owner[:, None]
    earlier = ranking[None, :] < ranking[:, None]
    position = jnp.sum((shared_owner & earlier).astype(jnp.int32), axis=1)
    return bin_owner * capacity + position


def slot_sources(targets, first_slot, slot_count):
    wanted = first_slot + jnp.arange(slot_count, dtype=jnp.int32)
    matches = targets[None, :] == wanted[:, None]
    bin_ids = jnp.arange(targets.shape[0], dtype=jnp.int32)
    sources = jnp.sum(jnp.where(matches, bin_ids[None, :], 0), axis=1)
    return (sources, jnp.any(matches, axis=1))


def shards(spectra, pair_bin, bin_owner):
    white = whiten(spectra)
    bin_count = bin_owner.shape[0]
    stacked = cross_bins(white, white, pair_bin[:, 0, :], bin_count)
    carried = white
    for reach_step in range(1, REACH + 1):
        carried = shifted(carried, "chan", -1)
        stacked = stacked + cross_bins(white, carried, pair_bin[:, reach_step, :], bin_count)
    targets = bin_slots(bin_owner, CAP)
    summed = lax.psum(stacked, "win")
    sources, present = slot_sources(targets, lax.axis_index("win") * CAP, CAP)
    owned = jnp.where(present[:, None, None], summed[sources], 0.0)
    factor = math.sqrt(
        BINS_OWN / (spectra.shape[1] * (REACH + 1) * spectra.shape[0] * spectra.shape[0])
    )
    return (owned * factor)[None]


def solution(mesh):
    in_specs = (P("chan", "win", None, None), P("chan", None, None), P())
    out_specs = P("chan", "win", None, None)
    return jax.shard_map(shards, mesh=mesh, in_specs=in_specs, out_specs=out_specs, check_vma=False)
```

profile of v0, /device:TPU:1, one launch (start us, length us, event | category | flops | bytes accessed | tf_op | source)
XLA Modules:
  0.0 474.8 jit_solution(13924063393163099408)
XLA Ops:
  6.5 0.0 all-reduce.2.cloned.1.call-start
  6.5 6.8 %copy.56 = bf16[8,16,2,1024]{1,0,2,3:T(8,128)(2,1)} copy(bf16[8,16,2,1024]{3,2,1,0:T(2,128)(2,1)} %param.3) | data formatting | bytes 1048576 | tf_op args[0]
  13.4 0.0 copy-start
  13.4 4.5 fusion
  17.9 0.0 copy-done
  17.9 2.8 fusion.1
  20.7 4.4 copy.60
  25.1 0.0 copy-start.1
  25.1 10.9 %collective-permute-start = (bf16[8,16,2,1024]{3,1,2,0:T(8,128)(2,1)S(1)}, bf16[8,16,2,1024]{3,1,2,0:T(8,128)(2,1)S(1)}, u32[]{:S(2)}, u32[]{:S(2)}) collective-permute-start(bf16[8,16,2,1024]{3,1,2,0:T(8,128)(2,1)S(1)} %copy.60), channel_id=1, source_target_pairs={{0,480},{32,0},{64,32},{96,64},{128,96},{160,128},{192,160},{224,1... | collective-permute-start | bytes 1572872 | tf_op jit(solution)/shard_map/ppermute | solution.py:15
  36.0 2.6 slice_negate_fusion
  38.6 0.0 copy-done.1
  38.6 2.7 fusion.56
  41.4 2.9 maximum_bitcast_fusion
  44.3 0.0 copy-start.2
  44.3 10.5 %fusion.27 = f32[8,8,2,1024]{0,1,2,3:T(8,128)} fusion(bf16[8,16,2,1024]{1,0,2,3:T(8,128)(2,1)} %fusion.1, bf16[8,16,2,1,1024]{1,0,2,3,4:T(8,128)(2,1)} %maximum_bitcast_fusion, bf16[8,16,2,1,1024]{1,0,2,3,4:T(8,128)(2,1)} %fusion.56), kind=kOutput, calls=%fused_computation.23 | convolution fusion | flops 8912896 | bytes 2097152 | tf_op jit(solution)/shard_map/awcf,bwcjf->abjf/dot_general | solution.py:28
  54.7 0.0 copy-done.2
  54.7 0.1 eq.77
  54.8 5.2 %copy.77 = f32[8,8,2,1024]{3,1,2,0:T(8,128)S(1)} copy(f32[8,8,2,1024]{0,1,2,3:T(8,128)} %fusion.27) | data formatting | bytes 1048576
  60.0 0.1 eq.81
  60.1 0.1 eq.85
  60.2 0.7 fusion.36
  60.9 0.0 collective-permute-done
  60.9 0.1 pad_maximum_fusion
  61.0 4.8 %copy.62 = bf16[8,16,2,1024]{1,0,2,3:T(8,128)(2,1)} copy(bf16[8,16,2,1024]{3,1,2,0:T(8,128)(2,1)S(1)} %pad_maximum_fusion) | data formatting | bytes 1048576 | tf_op jit(solution)/shard_map/stack | solution.py:26
  65.7 4.7 copy.61
  70.5 2.1 collective-permute-start.1
  72.6 10.5 %fusion.22 = f32[8,8,2,1024]{0,1,2,3:T(8,128)} fusion(bf16[8,16,2,1024]{1,0,2,3:T(8,128)(2,1)} %fusion.1, bf16[8,16,2,1,1024]{1,0,2,3,4:T(8,128)(2,1)} %bitcast.99, bf16[8,16,2,1,1024]{1,0,2,3,4:T(8,128)(2,1)} %bitcast.100), kind=kOutput, calls=%fused_computation.22 | convolution fusion | flops 8912896 | bytes 2097152 | tf_op jit(solution)/shard_map/awcf,bwcjf->abjf/dot_general | solution.py:28
  83.0 5.9 %copy.78 = f32[8,8,2,1024]{3,1,2,0:T(8,128)} copy(f32[8,8,2,1024]{0,1,2,3:T(8,128)} %fusion.22) | data formatting | bytes 1048576
  88.9 1.7 convolution_add_fusion.1
  90.7 0.0 collective-permute-done.1
  90.7 0.1 pad_maximum_fusion.1
  90.8 4.8 %copy.66 = bf16[8,16,2,1024]{1,0,2,3:T(8,128)(2,1)} copy(bf16[8,16,2,1024]{3,1,2,0:T(8,128)(2,1)S(1)} %pad_maximum_fusion.1) | data formatting | bytes 1048576 | tf_op jit(solution)/shard_map/stack | solution.py:26
  95.5 4.7 copy.65
  100.3 10.5 %fusion.17 = f32[8,8,2,1024]{0,1,2,3:T(8,128)} fusion(bf16[8,16,2,1024]{1,0,2,3:T(8,128)(2,1)} %fusion.1, bf16[8,16,2,1,1024]{1,0,2,3,4:T(8,128)(2,1)} %bitcast.101, bf16[8,16,2,1,1024]{1,0,2,3,4:T(8,128)(2,1)} %bitcast.102), kind=kOutput, calls=%fused_computation.21 | convolution fusion | flops 8912896 | bytes 2097152 | tf_op jit(solution)/shard_map/awcf,bwcjf->abjf/dot_general | solution.py:28
  110.7 0.0 copy-start.3
  110.7 5.2 %copy.79 = f32[8,8,2,1024]{3,1,2,0:T(8,128)S(1)} copy(f32[8,8,2,1024]{0,1,2,3:T(8,128)} %fusion.17) | data formatting | bytes 1048576
  115.9 1.7 convolution_add_fusion
  117.6 0.0 all-reduce.2.cloned.1.call-update
  117.7 0.0 copy-done.3
  117.7 0.2 convert_reduce_fusion
  117.9 0.2 fusion.50
  118.1 0.2 compare_reduce_fusion
  118.3 346.3 %all-reduce.2.cloned.1.call-done = f32[128,2,1024]{2,0,1:T(8,128)} async-done(((f32[128,2,1024]{2,0,1:T(8,128)}), f32[128,2,1024]{2,0,1:T(8,128)}) %all-reduce.2.cloned.1.call-update) | async-done | bytes 1048592 | tf_op jit(solution)/shard_map/psum | solution.py:66
  464.5 2.0 copy.69
  466.6 0.6 gather_fusion
  467.2 0.7 fusion.40
  (8 shorter events, 0.1 us)
Async XLA Ops:
  6.5 458.0 %all-reduce.2.cloned.1.call-start = ((), (), s32[]{:S(2)}) async-start(), calls=%async_computation | async-start | bytes 2097152 | tf_op jit(solution)/shard_map/psum | solution.py:66
  13.4 4.5 copy-start
  25.1 13.6 %copy-start.1 = (bf16[8,16,2,1024]{1,0,2,3:T(8,128)(2,1)S(1)}, bf16[8,16,2,1024]{1,0,2,3:T(8,128)(2,1)}, u32[]{:S(2)}) copy-start(bf16[8,16,2,1024]{1,0,2,3:T(8,128)(2,1)} %copy.56) | copy-start | bytes 1572868
  25.1 35.8 %collective-permute-start = (bf16[8,16,2,1024]{3,1,2,0:T(8,128)(2,1)S(1)}, bf16[8,16,2,1024]{3,1,2,0:T(8,128)(2,1)S(1)}, u32[]{:S(2)}, u32[]{:S(2)}) collective-permute-start(bf16[8,16,2,1024]{3,1,2,0:T(8,128)(2,1)S(1)} %copy.60), channel_id=1, source_target_pairs={{0,480},{32,0},{64,32},{96,64},{128,96},{160,128},{192,160},{224,1... | collective-permute-start | bytes 1572872 | tf_op jit(solution)/shard_map/ppermute | solution.py:15
  44.3 10.5 %copy-start.2 = (s32[8,3,8]{2,0,1:T(8,128)S(1)}, s32[8,3,8]{2,0,1:T(8,128)}, u32[]{:S(2)}) copy-start(s32[8,3,8]{2,0,1:T(8,128)} %param.4) | copy-start | bytes 2308
  70.5 20.2 %collective-permute-start.1 = (bf16[8,16,2,1024]{3,1,2,0:T(8,128)(2,1)S(1)}, bf16[8,16,2,1024]{3,1,2,0:T(8,128)(2,1)S(1)}, u32[]{:S(2)}, u32[]{:S(2)}) collective-permute-start(bf16[8,16,2,1024]{3,1,2,0:T(8,128)(2,1)S(1)} %collective-permute-done), channel_id=1, source_target_pairs={{0,480},{32,0},{64,32},{96,64},{128,96},{160,128},{192,160},{224,1... | collective-permute-start | bytes 1572872 | tf_op jit(solution)/shard_map/ppermute | solution.py:15
  110.7 7.0 %copy-start.3 = (s32[128]{0:T(128)S(1)}, s32[128]{0:T(128)}, u32[]{:S(2)}) copy-start(s32[128]{0:T(128)} %param.5) | copy-start | bytes 1540
Sparse Core Ops, SparseCore 0:
  117.8 346.6 all-reduce.1
where the time goes:
time: 475 us
  waiting for transfers between devices  346 us (73%)
  local copies, waits for them, and re-layouts  49.4 us (10%)
  matrix products  35.5 us (7%)
  other arithmetic  17 us (4%)
  between operations  13.6 us (3%)
  starting transfers between devices  13 us (3%)
    psum x1, waiting for transfers between devices, shards(): summed = lax.psum(stacked, 'win')  346 us
    dot_general x3, matrix products, cross_bins(): jnp.einsum('awcf,bwcjf->abjf', near_block, partner, preferred_element_typ...  31.4 us
    unnamed x12, local copies, waits for them, and re-layouts  23.1 us
    ppermute x2, starting transfers between devices, shifted(): lax.ppermute(shard, axis, [(i, (i + by) % size) for i in range(size)])  13 us
    another operation x2, local copies, waits for them, and re-layouts, cross_bins(): rotated = jnp.stack([-far_block[:, :, 1], far_block[:, :, 0]], axis=2)  9.53 us
  transfers between devices with their start and end apart: 3, of which 1 were waited for; matrix products, arithmetic and copies ran while one was open for 9% of the time, Pallas kernels for 0%

commit v1 on v0

v1 whole, which is shorter than its diff:
```python
import functools
import math

import jax
import jax.numpy as jnp
from jax import lax
from jax.experimental import pallas as pl
from jax.experimental.pallas import tpu as pltpu
from jax.sharding import PartitionSpec as P

REACH = 2
BINS_OWN = 4
CAP = 7
EPS = 1e-06
F32 = jnp.float32
BF16 = jnp.bfloat16


def kernel(
    n_chan, factor,
    spec_ref, pair_ref, owner_ref, out_ref,
    white, afull, near1, near2, tmp, prods, selt, sel, pick, stack, cbuf,
    ysend, yrecv, yacc, zrecv, ufull, vslots, rbuf,
    s1, r1, s2, r2, cs, cr, ys, yr, zs, zr, us, ur, fs, fr,
):
    chan = lax.axis_index("chan")
    win = lax.axis_index("win")
    chip = win // 2
    core = win % 2
    y = chip // 2
    zh = chip % 2
    left = (chan + n_chan - 1) % n_chan
    right = (chan + 1) % n_chan
    sibling = win + 1 - 2 * core
    mesh_id = pl.DeviceIdType.MESH
    mine = pl.multiple_of(core * 64, 64)
    theirs = pl.multiple_of((1 - core) * 64, 64)

    barrier = pltpu.get_barrier_semaphore()
    for near in (left, right):
        pl.semaphore_signal(barrier, inc=1, device_id=(near, win), device_id_type=mesh_id)
    pl.semaphore_signal(barrier, inc=1, device_id=(chan, sibling), device_id_type=mesh_id)
    for o in range(1, 16):
        pl.semaphore_signal(
            barrier, inc=1, device_id=(chan, ((chip + o) % 16) * 2 + core), device_id_type=mesh_id
        )
    pl.semaphore_wait(barrier, 18)

    def remote(src, dst, send, recv, to):
        return pltpu.make_async_remote_copy(
            src_ref=src, dst_ref=dst, send_sem=send, recv_sem=recv, device_id=to, device_id_type=mesh_id
        )

    def hop1(k):
        return remote(white.at[k], near1.at[k], s1.at[k], r1.at[k], (left, win))

    def hop2(k):
        return remote(near1.at[k], near2.at[k], s2.at[k], r2.at[k], (left, win))

    def whiten(c, carry):
        x = spec_ref[c].astype(F32)
        power = jnp.sum(jnp.sum(x * x, axis=1, keepdims=True), axis=2, keepdims=True) * (1.0 / 2048.0)
        v = x * lax.rsqrt(power + EPS)
        tmp[...] = v.reshape(256, 128)
        re = tmp[pl.ds(0, 128, stride=2), :].reshape(16, 8, 128)
        im = tmp[pl.ds(1, 128, stride=2), :].reshape(16, 8, 128)
        wb = jnp.concatenate([re, im], axis=1).astype(BF16)
        white[c] = wb
        afull[c] = wb.astype(F32)
        hop1(c).start()
        return carry

    lax.fori_loop(0, 8, whiten, 0)

    def products(far, k):
        re = [None] * 8
        im = [None] * 8
        for w in range(16):
            b = far[k, w].astype(F32)
            br, bi = b[:8], b[8:]
            for c in range(8):
                ar = afull[c, w, 0:8, :]
                ai = afull[c, w, 8:16, :]
                pr = ar * br + ai * bi
                pi = ai * br - ar * bi
                re[c] = pr if w == 0 else re[c] + pr
                im[c] = pi if w == 0 else im[c] + pi
        for c in range(8):
            row = pl.multiple_of((k * 8 + c) * 16, 16)
            prods[pl.ds(row, 8), :] = re[c]
            prods[pl.ds(row + 8, 8), :] = im[c]

    def gather_bins(d, h):
        rows = jnp.concatenate(
            [prods[pl.ds(2 * h, 64, stride=16), :], prods[pl.ds(2 * h + 1, 64, stride=16), :]], axis=1
        )
        hi = rows.astype(BF16)
        lo = (rows - hi.astype(F32)).astype(BF16)
        both = jnp.concatenate([hi, lo], axis=0)
        t = jnp.dot(sel[d], both, preferred_element_type=F32)
        if d == 0:
            stack[2 * h] = t[:, :128]
            stack[2 * h + 1] = t[:, 128:]
        else:
            stack[2 * h] += t[:, :128]
            stack[2 * h + 1] += t[:, 128:]

    lanes = lax.broadcasted_iota(jnp.int32, (1, 128), 1)
    for d in range(REACH + 1):
        def fill(j, carry, d=d):
            hit = jnp.where(lanes == pair_ref[j % 8, d, j // 8], 1.0, 0.0)
            selt[pl.ds(j, 1), :] = hit
            selt[pl.ds(j + 64, 1), :] = hit
            return carry

        lax.fori_loop(0, 64, fill, 0)
        sel[d] = selt[...].T.astype(BF16)

    def own(k, carry):
        products(white, k)
        return carry

    lax.fori_loop(0, 8, own, 0)
    for h in range(8):
        gather_bins(0, h)

    def step1(k, carry):
        hop1(k).wait_recv()
        hop2(k).start()
        products(near1, k)
        return carry

    lax.fori_loop(0, 8, step1, 0)
    for h in range(8):
        gather_bins(1, h)

    owner = owner_ref[...]
    across = jnp.broadcast_to(owner.astype(F32), (128, 128))
    down = across.T
    rows_i = lax.broadcasted_iota(jnp.int32, (128, 128), 0)
    cols_i = lax.broadcasted_iota(jnp.int32, (128, 128), 1)
    ahead = jnp.where((across == down) & (rows_i < cols_i), 1.0, 0.0)
    rank = jnp.sum(ahead, axis=0, keepdims=True)
    slot = owner.astype(F32) * 8.0 + rank
    wanted = ((rows_i >> 3) * 2 + core) * 8 + (rows_i & 7)
    pick[...] = jnp.where(wanted.astype(F32) == slot, 1.0, 0.0)

    def step2(k, carry):
        hop2(k).wait_recv()
        products(near2, k)
        return carry

    lax.fori_loop(0, 8, step2, 0)

    def core_copy(h):
        return remote(
            stack.at[pl.ds(2 * h, 2), pl.ds(theirs, 64), :], cbuf.at[pl.ds(2 * h, 2)],
            cs.at[h], cr.at[h], (chan, sibling),
        )

    for h in range(8):
        gather_bins(2, h)
        core_copy(h).start()

    def y_copy(o):
        to = (y + o) % 8
        return remote(
            ysend.at[o - 1], yrecv.at[o - 1], ys.at[o - 1], yr.at[o - 1],
            (chan, to * 4 + zh * 2 + core),
        )

    scale = 1.0 + chip.astype(F32) * 0.0625
    acc = None
    for o in (4, 3, 5, 2, 6, 1, 7, 0):
        h = (y + o) % 8
        core_copy(h).wait_recv()
        t = stack[pl.ds(2 * h, 2), pl.ds(mine, 64), :] + cbuf[pl.ds(2 * h, 2)]
        if o:
            ysend[o - 1] = (t * scale).astype(BF16)
            y_copy(o).start()
        else:
            acc = t
    for o in (1, 7, 2, 6, 3, 5, 4):
        source = ((y + 8 - o) % 8) * 2 + zh
        y_copy(o).wait_recv()
        acc = acc + yrecv[o - 1].astype(F32) * (1.0 / (1.0 + source.astype(F32) * 0.0625))
    yacc[...] = acc
    z_copy = remote(yacc.at[1 - zh], zrecv, zs, zr, (chan, y * 4 + (1 - zh) * 2 + core))
    z_copy.start()
    z_copy.wait_recv()
    ufull[pl.ds(mine, 64), :] = yacc[zh] + zrecv[...]
    u_copy = remote(ufull.at[pl.ds(mine, 64)], ufull.at[pl.ds(mine, 64)], us, ur, (chan, sibling))
    u_copy.start()
    u_copy.wait_recv()
    v = jnp.dot(pick[...], ufull[...], precision=lax.Precision.HIGHEST, preferred_element_type=F32)
    vslots[...] = (v * factor).reshape(16, 8, 128)

    def slot_copy(o, src, dst, to):
        return remote(vslots.at[src], rbuf.at[dst], fs.at[o - 1], fr.at[o - 1], (chan, to * 2 + core))

    for o in range(1, 16):
        to = (chip + o) % 16
        slot_copy(o, to, chip, to).start()
    rbuf[chip] = vslots[chip]
    for o in range(1, 16):
        slot_copy(o, (chip + o) % 16, (chip + 16 - o) % 16, (chip + o) % 16).wait_recv()
    out_ref[...] = rbuf[...]

    for k in range(8):
        hop1(k).wait_send()
        hop2(k).wait_send()
        core_copy(k).wait_send()
    for o in range(1, 8):
        y_copy(o).wait_send()
    z_copy.wait_send()
    u_copy.wait_send()
    for o in range(1, 16):
        to = (chip + o) % 16
        slot_copy(o, to, chip, to).wait_send()


def shards(n_chan, spectra, pair_bin, bin_owner):
    channels, windows, _, freqs = spectra.shape
    factor = math.sqrt(BINS_OWN / (windows * (REACH + 1) * channels * channels))
    rows = spectra.reshape(channels, windows, 2, freqs // 128, 128)
    rows = rows.transpose(0, 1, 3, 2, 4).reshape(channels, windows, 16, 128)
    vmem = pl.BlockSpec(memory_space=pltpu.VMEM)
    dma = pltpu.SemaphoreType.DMA
    block = (8, 16, 16, 128)
    out = pl.pallas_call(
        functools.partial(kernel, n_chan, factor),
        out_shape=jax.ShapeDtypeStruct((16, 8, 128), F32),
        in_specs=[vmem, pl.BlockSpec(memory_space=pltpu.SMEM), vmem],
        out_specs=vmem,
        scratch_shapes=[
            pltpu.VMEM(block, BF16),
            pltpu.VMEM(block, F32),
            pltpu.VMEM(block, BF16),
            pltpu.VMEM(block, BF16),
            pltpu.VMEM((256, 128), F32),
            pltpu.VMEM((1024, 128), F32),
            pltpu.VMEM((128, 128), F32),
            pltpu.VMEM((3, 128, 128), BF16),
            pltpu.VMEM((128, 128), F32),
            pltpu.VMEM((16, 128, 128), F32),
            pltpu.VMEM((16, 64, 128), F32),
            pltpu.VMEM((7, 2, 64, 128), BF16),
            pltpu.VMEM((7, 2, 64, 128), BF16),
            pltpu.VMEM((2, 64, 128), F32),
            pltpu.VMEM((64, 128), F32),
            pltpu.VMEM((128, 128), F32),
            pltpu.VMEM((16, 8, 128), F32),
            pltpu.VMEM((16, 8, 128), F32),
            dma((8,)), dma((8,)), dma((8,)), dma((8,)), dma((8,)), dma((8,)),
            dma((7,)), dma((7,)), dma, dma, dma, dma, dma((15,)), dma((15,)),
        ],
        compiler_params=pltpu.CompilerParams(
            collective_id=0, has_side_effects=True, vmem_limit_bytes=32 * 1024 * 1024
        ),
    )(rows, pair_bin, bin_owner.reshape(1, 128))
    out = out[:, :CAP].reshape(2, 8, CAP, 128).transpose(2, 0, 1, 3)
    return out.reshape(1, CAP, 2, freqs)


def solution(mesh):
    in_specs = (P("chan", "win", None, None), P("chan", None, None), P())
    out_specs = P("chan", "win", None, None)
    body = functools.partial(shards, mesh.shape["chan"])
    return jax.shard_map(body, mesh=mesh, in_specs=in_specs, out_specs=out_specs, check_vma=False)
```

time: 475 us -> 67.5 us (0.14)
  waiting for transfers between devices: 346 us -> 0 us
  Pallas kernels: 0 us -> 64.8 us
  local copies, waits for them, and re-layouts: 49.4 us -> 2.43 us
  matrix products: 35.5 us -> 0 us
  other arithmetic: 17 us -> 0 us
  between operations: 13.6 us -> 0.02 us
  starting transfers between devices: 13 us -> 0 us
    psum x1 -> x0, waiting for transfers between devices: 346 us -> none  [shards(): summed = lax.psum(stacked, 'win')]
    pallas_call x0 -> x1, Pallas kernels: none -> 64.8 us  [shards(): pl.pallas_call(functools.partial(kernel, n_chan, factor), out_shape=jax.S...]
    dot_general x6 -> x0, matrix products: 35.5 us -> none  [the longest x3 31.4 us: cross_bins(): jnp.einsum('awcf,bwcjf->abjf', near_block, partner, preferred_element_typ...]
    unnamed x12 -> x5, local copies, waits for them, and re-layouts: 23.1 us -> 1.77 us
    ppermute x2 -> x0, starting transfers between devices: 13 us -> none  [shifted(): lax.ppermute(shard, axis, [(i, (i + by) % size) for i in range(size)])]
    another operation x2 -> x0, local copies, waits for them, and re-layouts: 9.53 us -> none  [cross_bins(): rotated = jnp.stack([-far_block[:, :, 1], far_block[:, :, 0]], axis=2)]
    ppermute x2 -> x0, local copies, waits for them, and re-layouts: 9.44 us -> none  [shifted(): lax.ppermute(shard, axis, [(i, (i + by) % size) for i in range(size)])]
    another operation x4 -> x0, other arithmetic: 5.75 us -> none  [the longest x2 5.64 us: cross_bins(): partner = jnp.stack([far_block, rotated], axis=3)]
  transfers between devices with their start and end apart: 3 -> 0, of which waited for: 1 -> 0; matrix products, arithmetic and copies ran while one was open for 9% -> 0% of each run, Pallas kernels for 0% -> 0%
where the time goes in v1:
time: 67.5 us; the launch traced here: 67.3 us
  Pallas kernels  64.8 us (96%)
  local copies, waits for them, and re-layouts  2.43 us (4%)
    pallas_call x1, Pallas kernels, shards(): pl.pallas_call(functools.partial(kernel, n_chan, factor), out_shape=jax.S...  64.8 us
    unnamed x5, local copies, waits for them, and re-layouts  1.77 us

profile of v1, /device:TPU:1, one launch (start us, length us, event | category | flops | bytes accessed | tf_op | source)
XLA Modules:
  0.0 67.3 jit_solution(2381946575107679833)
XLA Ops:
  0.0 0.0 copy-start.1
  0.0 0.7 %copy.5.pair_ref = s32[8,3,8]{2,1,0:T(4,128)S(1)} copy(s32[8,3,8]{2,0,1:T(8,128)} %param.4) | data formatting | bytes 1536 | tf_op args[1]
  0.7 0.0 copy-done.1
  0.7 0.0 copy-start
  0.7 1.0 %copy-done = bf16[8,16,2,1024]{3,2,1,0:T(2,128)(2,1)S(1)} copy-done((bf16[8,16,2,1024]{3,2,1,0:T(2,128)(2,1)S(1)}, bf16[8,16,2,1024]{3,2,1,0:T(2,128)(2,1)}, u32[]{:S(2)}) %copy-start) | copy-done | bytes 524312
  1.8 64.8 %shard_map.37 = f32[16,8,128]{2,1,0:T(8,128)S(1)} custom-call(bf16[8,16,16,128]{3,2,1,0:T(8,128)(2,1)S(1)} %bitcast.12, s32[8,3,8]{2,1,0:T(4,128)S(1)} %copy.5.pair_ref, s32[1,128]{1,0:T(1,128)S(1)} %bitcast.14), custom_call_target="tpu_custom_call" | custom-call | tf_op jit(solution)/shard_map/pallas_call | solution.py:230
  66.6 0.7 reshape.19
  (1 shorter events, 0.0 us)
Async XLA Ops:
  0.0 0.7 %copy-start.1 = (s32[128]{0:T(128)S(1)}, s32[128]{0:T(128)}, u32[]{:S(2)}) copy-start(s32[128]{0:T(128)} %param.5) | copy-start | bytes 1540
  0.7 1.0 %copy-start = (bf16[8,16,2,1024]{3,2,1,0:T(2,128)(2,1)S(1)}, bf16[8,16,2,1024]{3,2,1,0:T(2,128)(2,1)}, u32[]{:S(2)}) copy-start(bf16[8,16,2,1024]{3,2,1,0:T(2,128)(2,1)} %param.3) | copy-start | bytes 1572868

commit v2 on v0

v2 whole, which is shorter than its diff:
```python
import functools
import math

import jax
import jax.numpy as jnp
from jax import lax
from jax.experimental import pallas as pl
from jax.experimental.pallas import tpu as pltpu
from jax.sharding import PartitionSpec as P

REACH = 2
BINS_OWN = 4
CAP = 7
EPS = 1e-06
CHUNK = 2
F32 = jnp.float32
BF16 = jnp.bfloat16
FAR_FIRST = (4, 3, 5, 2, 6, 1, 7)


def kernel(
    n_chan, factor,
    spec_hbm, pair_ref, owner_ref, out_ref,
    spec, tmp, wsend, full, afull, near1, near2, prods, selt, sel, pick, stack, cbuf, vslots, rbuf,
    ins, ats, atr, s1, r1, s2, r2, cs, cr, fs, fr,
):
    chan = lax.axis_index("chan")
    win = lax.axis_index("win")
    core = win % 2
    y = win // 4
    inner = win % 4
    left = (chan + n_chan - 1) % n_chan
    right = (chan + 1) % n_chan
    sibling = win + 1 - 2 * core
    mesh_id = pl.DeviceIdType.MESH

    barrier = pltpu.get_barrier_semaphore()
    for near in (left, right):
        pl.semaphore_signal(barrier, inc=1, device_id=(near, win), device_id_type=mesh_id)
    for o in range(1, 32):
        pl.semaphore_signal(barrier, inc=1, device_id=(chan, (win + o) % 32), device_id_type=mesh_id)

    def load(c):
        return pltpu.make_async_copy(spec_hbm.at[c], spec.at[c], ins.at[c])

    for c in range(8):
        load(c).start()

    def remote(src, dst, send, recv, to):
        return pltpu.make_async_remote_copy(
            src_ref=src, dst_ref=dst, send_sem=send, recv_sem=recv, device_id=to, device_id_type=mesh_id
        )

    def spread(j, o, origin):
        to = (y + o) % 8
        rows = pl.multiple_of(origin * 16, 16)
        n = j * 7 + o - 1
        return remote(
            wsend.at[to, pl.ds(CHUNK * j, CHUNK)],
            full.at[pl.ds(CHUNK * j, CHUNK), :, pl.ds(rows, 16), :],
            ats.at[n], atr.at[n], (chan, to * 4 + inner),
        )

    def hop1(k):
        return remote(full.at[k], near1.at[k], s1.at[k], r1.at[k], (left, win))

    def hop2(k):
        return remote(near1.at[k], near2.at[k], s2.at[k], r2.at[k], (left, win))

    def whiten(c):
        load(c).wait()
        x = spec[c].astype(F32)
        power = jnp.sum(jnp.sum(x * x, axis=1, keepdims=True), axis=2, keepdims=True) * (1.0 / 2048.0)
        tmp[c % 2] = (x * lax.rsqrt(power + EPS)).reshape(256, 128)
        for t in range(8):
            for p in range(2):
                wsend[t, c, p] = tmp[c % 2, pl.ds(2 * t + p, 16, stride=16), :].astype(BF16)

    own_rows = pl.multiple_of(y * 16, 16)
    for j in range(8 // CHUNK):
        for c in range(CHUNK * j, CHUNK * j + CHUNK):
            whiten(c)
        if j == 0:
            pl.semaphore_wait(barrier, 33)
        for o in FAR_FIRST:
            spread(j, o, y).start()
        part = slice(CHUNK * j, CHUNK * j + CHUNK)
        full[part, :, pl.ds(own_rows, 16), :] = wsend[y, part]

    lanes = lax.broadcasted_iota(jnp.int32, (8, 128), 1)

    def select(d):
        def fill(j, carry):
            row = pl.multiple_of(j * 8, 8)
            selt[pl.ds(row, 8), :] = jnp.where(lanes == pair_ref[d, j % 8, j // 8], 1.0, 0.0)
            return carry

        lax.fori_loop(0, 64, fill, 0)
        sel[d] = selt[...].T.astype(BF16)

    for j in range(8 // CHUNK):
        if j < REACH + 1:
            select(j)
        for o in FAR_FIRST[::-1]:
            spread(j, o, (y + 8 - o) % 8).wait_recv()
        for k in range(CHUNK * j, CHUNK * j + CHUNK):
            hop1(k).start()
        if j:
            for k in range(CHUNK * j - CHUNK, CHUNK * j):
                hop1(k).wait_recv()
                hop2(k).start()
        part = slice(CHUNK * j, CHUNK * j + CHUNK)
        afull[part] = full[part].astype(F32)

    def products(far, k):
        re = [None] * 8
        im = [None] * 8
        for g in range(8):
            wide_r = far[k, 0, 16 * g:16 * g + 16, :].astype(F32)
            wide_i = far[k, 1, 16 * g:16 * g + 16, :].astype(F32)
            for h in range(2):
                br, bi = wide_r[8 * h:8 * h + 8], wide_i[8 * h:8 * h + 8]
                w = 16 * g + 8 * h
                for c in range(8):
                    ar = afull[c, 0, w:w + 8, :]
                    ai = afull[c, 1, w:w + 8, :]
                    pr = ar * br + ai * bi
                    pi = ai * br - ar * bi
                    re[c] = pr if w == 0 else re[c] + pr
                    im[c] = pi if w == 0 else im[c] + pi
        for c in range(8):
            row = pl.multiple_of((k * 8 + c) * 8, 8)
            prods[0, pl.ds(row, 8), :] = re[c]
            prods[1, pl.ds(row, 8), :] = im[c]

    def gather_bins(d):
        rows = jnp.concatenate([prods[0], prods[1]], axis=1)
        hi = rows.astype(BF16)
        lo = (rows - hi.astype(F32)).astype(BF16)
        t = jnp.dot(sel[d], hi, preferred_element_type=F32) + jnp.dot(sel[d], lo, preferred_element_type=F32)
        if d == 0:
            stack[0] = t[:, :128]
            stack[1] = t[:, 128:]
        else:
            stack[0] += t[:, :128]
            stack[1] += t[:, 128:]

    for k in range(8 - CHUNK, 8):
        hop1(k).wait_recv()
        hop2(k).start()

    def own(k, carry):
        products(full, k)
        return carry

    lax.fori_loop(0, 8, own, 0)
    gather_bins(0)

    def step1(k, carry):
        products(near1, k)
        return carry

    lax.fori_loop(0, 8, step1, 0)
    gather_bins(1)

    owner = owner_ref[...].astype(F32)
    across = jnp.broadcast_to(owner, (128, 128))
    down = across.T
    rows_i = lax.broadcasted_iota(jnp.int32, (128, 128), 0)
    cols_i = lax.broadcasted_iota(jnp.int32, (128, 128), 1)
    ahead = jnp.where((across == down) & (rows_i < cols_i), 1.0, 0.0)
    slot = owner * 8.0 + jnp.sum(ahead, axis=0, keepdims=True)
    wanted = lax.broadcasted_iota(jnp.int32, (256, 128), 0).astype(F32)
    hit = jnp.where(wanted == slot, 1.0, 0.0).astype(BF16)
    pick[...] = jnp.concatenate([hit, hit], axis=1)

    def step2(k, carry):
        hop2(k).wait_recv()
        products(near2, k)
        return carry

    lax.fori_loop(0, 8, step2, 0)
    gather_bins(2)

    core_copy = remote(stack.at[1 - core], cbuf, cs, cr, (chan, sibling))
    core_copy.start()
    core_copy.wait_recv()
    total = (stack[core] + cbuf[...]) * factor
    hi = total.astype(BF16)
    lo = (total - hi.astype(F32)).astype(BF16)
    v = jnp.dot(pick[...], jnp.concatenate([hi, lo], axis=0), preferred_element_type=F32)
    vslots[...] = v.reshape(32, 8, 128)

    def slot_copy(o, origin):
        to = (win + o) % 32
        return remote(vslots.at[to], rbuf.at[origin], fs.at[o - 1], fr.at[o - 1], (chan, to))

    def send_slots(i, carry):
        o = (i + 16) % 31 + 1
        slot_copy(o, win).start()
        return carry

    lax.fori_loop(0, 31, send_slots, 0)
    rbuf[win] = vslots[win]

    def take_slots(i, carry):
        o = i + 1
        slot_copy(o, (win + 32 - o) % 32).wait_recv()
        return carry

    lax.fori_loop(0, 31, take_slots, 0)
    for t in range(8):
        for p in range(2):
            out_ref[p * 8 + t] = rbuf[t * 4 + p] + rbuf[t * 4 + 2 + p]

    for j in range(8 // CHUNK):
        for o in FAR_FIRST:
            spread(j, o, y).wait_send()
    for k in range(8):
        hop1(k).wait_send()
        hop2(k).wait_send()
    core_copy.wait_send()

    def finish(i, carry):
        slot_copy(i + 1, win).wait_send()
        return carry

    lax.fori_loop(0, 31, finish, 0)


def shards(n_chan, spectra, pair_bin, bin_owner):
    channels, windows, _, freqs = spectra.shape
    factor = math.sqrt(BINS_OWN / (windows * (REACH + 1) * channels * channels))
    rows = spectra.reshape(channels, windows, 2, freqs // 128, 128)
    rows = rows.transpose(0, 1, 3, 2, 4).reshape(channels, windows, 16, 128)
    vmem = pl.BlockSpec(memory_space=pltpu.VMEM)
    dma = pltpu.SemaphoreType.DMA
    block = (8, 2, 128, 128)
    out = pl.pallas_call(
        functools.partial(kernel, n_chan, factor),
        out_shape=jax.ShapeDtypeStruct((16, 8, 128), F32),
        in_specs=[pl.BlockSpec(memory_space=pl.ANY), pl.BlockSpec(memory_space=pltpu.SMEM), vmem],
        out_specs=vmem,
        scratch_shapes=[
            pltpu.VMEM((8, 16, 16, 128), BF16),
            pltpu.VMEM((2, 256, 128), F32),
            pltpu.VMEM((8, 8, 2, 16, 128), BF16),
            pltpu.VMEM(block, BF16),
            pltpu.VMEM(block, F32),
            pltpu.VMEM(block, BF16),
            pltpu.VMEM(block, BF16),
            pltpu.VMEM((2, 512, 128), F32),
            pltpu.VMEM((512, 128), F32),
            pltpu.VMEM((3, 128, 512), BF16),
            pltpu.VMEM((256, 256), BF16),
            pltpu.VMEM((2, 128, 128), F32),
            pltpu.VMEM((128, 128), F32),
            pltpu.VMEM((32, 8, 128), F32),
            pltpu.VMEM((32, 8, 128), F32),
            dma((8,)), dma((28,)), dma((28,)), dma((8,)), dma((8,)), dma((8,)), dma((8,)),
            dma, dma, dma((31,)), dma((31,)),
        ],
        compiler_params=pltpu.CompilerParams(
            collective_id=0, has_side_effects=True, vmem_limit_bytes=32 * 1024 * 1024
        ),
    )(rows, pair_bin.transpose(1, 0, 2), bin_owner.reshape(1, 128))
    out = out[:, :CAP].reshape(2, 8, CAP, 128).transpose(2, 0, 1, 3)
    return out.reshape(1, CAP, 2, freqs)


def solution(mesh):
    in_specs = (P("chan", "win", None, None), P("chan", None, None), P())
    out_specs = P("chan", "win", None, None)
    body = functools.partial(shards, mesh.shape["chan"])
    return jax.shard_map(body, mesh=mesh, in_specs=in_specs, out_specs=out_specs, check_vma=False)
```

time: 475 us -> 59.1 us (0.12)
  waiting for transfers between devices: 346 us -> 0 us
  Pallas kernels: 0 us -> 55.8 us
  local copies, waits for them, and re-layouts: 49.4 us -> 3.07 us
  matrix products: 35.5 us -> 0 us
  other arithmetic: 17 us -> 0 us
  between operations: 13.6 us -> 0.02 us
  starting transfers between devices: 13 us -> 0 us
    psum x1 -> x0, waiting for transfers between devices: 346 us -> none  [shards(): summed = lax.psum(stacked, 'win')]
    pallas_call x0 -> x1, Pallas kernels: none -> 55.8 us  [shards(): pl.pallas_call(functools.partial(kernel, n_chan, factor), out_shape=jax.S...]
    dot_general x6 -> x0, matrix products: 35.5 us -> none  [the longest x3 31.4 us: cross_bins(): jnp.einsum('awcf,bwcjf->abjf', near_block, partner, preferred_element_typ...]
    unnamed x12 -> x6, local copies, waits for them, and re-layouts: 23.1 us -> 2.4 us
    ppermute x2 -> x0, starting transfers between devices: 13 us -> none  [shifted(): lax.ppermute(shard, axis, [(i, (i + by) % size) for i in range(size)])]
    another operation x2 -> x0, local copies, waits for them, and re-layouts: 9.53 us -> none  [cross_bins(): rotated = jnp.stack([-far_block[:, :, 1], far_block[:, :, 0]], axis=2)]
    ppermute x2 -> x0, local copies, waits for them, and re-layouts: 9.44 us -> none  [shifted(): lax.ppermute(shard, axis, [(i, (i + by) % size) for i in range(size)])]
    another operation x4 -> x0, other arithmetic: 5.75 us -> none  [the longest x2 5.64 us: cross_bins(): partner = jnp.stack([far_block, rotated], axis=3)]
  transfers between devices with their start and end apart: 3 -> 0, of which waited for: 1 -> 0; matrix products, arithmetic and copies ran while one was open for 9% -> 0% of each run, Pallas kernels for 0% -> 0%
where the time goes in v2:
time: 59.1 us; the launch traced here: 58.9 us
  Pallas kernels  55.8 us (94%)
  local copies, waits for them, and re-layouts  3.07 us (5%)
    pallas_call x1, Pallas kernels, shards(): pl.pallas_call(functools.partial(kernel, n_chan, factor), out_shape=jax.S...  55.8 us
    unnamed x6, local copies, waits for them, and re-layouts  2.4 us

profile of v2, /device:TPU:1, one launch (start us, length us, event | category | flops | bytes accessed | tf_op | source)
XLA Modules:
  0.0 58.9 jit_solution(9685420407577091235)
XLA Ops:
  0.0 0.0 copy-start.2
  0.0 0.7 %copy-done.2 = s32[128]{0:T(128)S(1)} copy-done((s32[128]{0:T(128)S(1)}, s32[128]{0:T(128)}, u32[]{:S(2)}) %copy-start.2) | copy-done | bytes 536
  0.7 0.0 copy-start
  0.7 1.0 %copy-done = bf16[8,16,2,1024]{3,2,1,0:T(2,128)(2,1)S(1)} copy-done((bf16[8,16,2,1024]{3,2,1,0:T(2,128)(2,1)S(1)}, bf16[8,16,2,1024]{3,2,1,0:T(2,128)(2,1)}, u32[]{:S(2)}) %copy-start) | copy-done | bytes 524312
  1.7 0.0 copy-start.1
  1.7 0.7 %copy-done.1 = s32[8,3,8]{2,0,1:T(8,128)S(1)} copy-done((s32[8,3,8]{2,0,1:T(8,128)S(1)}, s32[8,3,8]{2,0,1:T(8,128)}, u32[]{:S(2)}) %copy-start.1) | copy-done | bytes 792
  2.4 55.8 %shard_map.37 = f32[16,8,128]{2,1,0:T(8,128)S(1)} custom-call(bf16[8,16,16,128]{3,2,1,0:T(8,128)(2,1)S(1)} %bitcast.13, s32[3,8,8]{2,1,0:T(8,128)S(1)} %bitcast.15, s32[1,128]{1,0:T(1,128)S(1)} %bitcast.16), custom_call_target="tpu_custom_call" | custom-call | tf_op jit(solution)/shard_map/pallas_call | solution.py:239
  58.3 0.7 %reshape.19 = f32[1,7,2,1024]{3,2,1,0:T(2,128)} reshape(f32[7,2,8,128]{3,2,1,0:T(8,128)S(1)} %copy.5) | data formatting | bytes 114688 | tf_op jit(solution)/shard_map/reshape | solution.py:268
  (1 shorter events, 0.0 us)
Async XLA Ops:
  0.0 0.7 %copy-start.2 = (s32[128]{0:T(128)S(1)}, s32[128]{0:T(128)}, u32[]{:S(2)}) copy-start(s32[128]{0:T(128)} %param.5) | copy-start | bytes 1540
  0.7 1.0 %copy-start = (bf16[8,16,2,1024]{3,2,1,0:T(2,128)(2,1)S(1)}, bf16[8,16,2,1024]{3,2,1,0:T(2,128)(2,1)}, u32[]{:S(2)}) copy-start(bf16[8,16,2,1024]{3,2,1,0:T(2,128)(2,1)} %param.3) | copy-start | bytes 1572868
  1.7 0.7 %copy-start.1 = (s32[8,3,8]{2,0,1:T(8,128)S(1)}, s32[8,3,8]{2,0,1:T(8,128)}, u32[]{:S(2)}) copy-start(s32[8,3,8]{2,0,1:T(8,128)} %param.4) | copy-start | bytes 2308

commit v3 on v0

v3 whole, which is shorter than its diff:
```python
import functools
import math

import jax
import jax.numpy as jnp
from jax import lax
from jax.experimental import pallas as pl
from jax.experimental.pallas import tpu as pltpu
from jax.sharding import PartitionSpec as P

REACH = 2
BINS_OWN = 4
CAP = 7
EPS = 1e-06
F32 = jnp.float32
BF16 = jnp.bfloat16
CHUNK = 2
PARTS = 8 // CHUNK
PACE = 4
LAG = 2
FAR_FIRST = (4, 3, 5, 2, 6, 1, 7)


def kernel(
    n_chan, factor,
    spec_hbm, pair_ref, owner_ref, out_ref,
    spec, tmp, wsend, full, afull, near1, near2, prods, selt, pick, comb, vbuf, cbuf, rbuf,
    ins, ats, atr, s1, r1, s2, r2, cs, cr, fs, fr,
):
    chan = lax.axis_index("chan")
    win = lax.axis_index("win")
    core = win % 2
    chip = win // 2
    y = chip // 2
    zh = chip % 2
    left = (chan + n_chan - 1) % n_chan
    right = (chan + 1) % n_chan
    sibling = win + 1 - 2 * core
    mesh_id = pl.DeviceIdType.MESH

    barrier = pltpu.get_barrier_semaphore()
    for near in (left, right):
        pl.semaphore_signal(barrier, inc=1, device_id=(near, win), device_id_type=mesh_id)
    pl.semaphore_signal(barrier, inc=1, device_id=(chan, sibling), device_id_type=mesh_id)
    for o in range(1, 16):
        pl.semaphore_signal(
            barrier, inc=1, device_id=(chan, ((chip + o) % 16) * 2 + core), device_id_type=mesh_id
        )

    def load(c):
        return pltpu.make_async_copy(spec_hbm.at[c], spec.at[c], ins.at[c])

    for c in range(8):
        load(c).start()

    def remote(src, dst, send, recv, to):
        return pltpu.make_async_remote_copy(
            src_ref=src, dst_ref=dst, send_sem=send, recv_sem=recv, device_id=to, device_id_type=mesh_id
        )

    def spread(j, o):
        to = (y + o) % 8
        part = slice(CHUNK * j, CHUNK * j + CHUNK)
        m = j * 7 + o - 1
        return remote(
            wsend.at[to, part], full.at[part, :, 16 * o:16 * o + 16, :],
            ats.at[m], atr.at[m], (chan, to * 4 + zh * 2 + core),
        )

    def cut(ref, j):
        if j == PARTS:
            return ref.at[:, :, 0:16, :]
        return ref.at[CHUNK * j:CHUNK * j + CHUNK, :, 16:128, :]

    def hop1(j):
        return remote(cut(full, j), cut(near1, j), s1.at[j], r1.at[j], (left, win))

    def hop2(j):
        return remote(cut(near1, j), cut(near2, j), s2.at[j], r2.at[j], (left, win))

    def whiten(c):
        load(c).wait()
        x = spec[c].astype(F32)
        power = jnp.sum(jnp.sum(x * x, axis=1, keepdims=True), axis=2, keepdims=True) * (1.0 / 2048.0)
        tmp[c % 2] = (x * lax.rsqrt(power + EPS)).reshape(256, 128)
        for t in range(8):
            for p in range(2):
                wsend[t, c, p] = tmp[c % 2, pl.ds(2 * t + p, 16, stride=16), :].astype(BF16)

    def send_part(j):
        for o in FAR_FIRST:
            spread(j, o).start()

    for j in range(PARTS):
        for c in range(CHUNK * j, CHUNK * j + CHUNK):
            whiten(c)
        if j == 0:
            pl.semaphore_wait(barrier, 18)
        if j < PACE:
            send_part(j)
    full[:, :, 0:16, :] = wsend[y]
    hop1(PARTS).start()

    lanes = lax.broadcasted_iota(jnp.int32, (8, 128), 1)

    def select(d):
        def fill(j, carry):
            row = pl.multiple_of(j * 8, 8)
            selt[d, pl.ds(row, 8), :] = jnp.where(lanes == pair_ref[d, j % 8, j // 8], 1.0, 0.0)
            return carry

        lax.fori_loop(0, 64, fill, 0)

    def find_slots():
        owner = owner_ref[...].astype(F32)
        across = jnp.broadcast_to(owner, (128, 128))
        down = across.T
        rows_i = lax.broadcasted_iota(jnp.int32, (128, 128), 0)
        cols_i = lax.broadcasted_iota(jnp.int32, (128, 128), 1)
        ahead = jnp.where((across == down) & (rows_i < cols_i), 1.0, 0.0)
        slot = owner * 8.0 + jnp.sum(ahead, axis=0, keepdims=True)
        r = lax.broadcasted_iota(jnp.int32, (256, 128), 0)
        wanted = (((r >> 3) & 7) * 4 + ((r >> 6) & 1) * 2 + (r >> 7)) * 8 + (r & 7)
        pick[...] = jnp.where(wanted.astype(F32) == slot, 1.0, 0.0).astype(BF16)

    def combine(d):
        comb[d] = jnp.dot(
            pick[...], selt[d].T.astype(BF16), preferred_element_type=F32
        ).astype(BF16)

    def products(d, far, part):
        def body(k, carry):
            re = [None] * 8
            im = [None] * 8
            for g in range(8):
                wide_r = far[k, 0, 16 * g:16 * g + 16, :].astype(F32)
                wide_i = far[k, 1, 16 * g:16 * g + 16, :].astype(F32)
                for h in range(2):
                    br, bi = wide_r[8 * h:8 * h + 8], wide_i[8 * h:8 * h + 8]
                    w = 16 * g + 8 * h
                    for c in range(8):
                        ar = afull[c, 0, w:w + 8, :]
                        ai = afull[c, 1, w:w + 8, :]
                        pr = ar * br + ai * bi
                        pi = ai * br - ar * bi
                        re[c] = pr if w == 0 else re[c] + pr
                        im[c] = pi if w == 0 else im[c] + pi
            for c in range(8):
                row = pl.multiple_of((k * 8 + c) * 8, 8)
                prods[d, 0, pl.ds(row, 8), :] = re[c]
                prods[d, 1, pl.ds(row, 8), :] = im[c]
            return carry

        lax.fori_loop(part.start, part.stop, body, 0)

    def slots_of(d):
        rows = jnp.concatenate([prods[d, 0], prods[d, 1]], axis=1)
        hi = rows.astype(BF16)
        lo = (rows - hi.astype(F32)).astype(BF16)
        return jnp.dot(comb[d], hi, preferred_element_type=F32) + jnp.dot(
            comb[d], lo, preferred_element_type=F32
        )

    def store_slots(v):
        for p in range(2):
            vbuf[:, :, :, p] = v[:, 128 * p:128 * p + 128].reshape(2, 2, 8, 8, 128)

    def forward(j):
        hop1(j).wait_recv()
        hop2(j).start()

    select(0)
    for j in range(PARTS):
        part = slice(CHUNK * j, CHUNK * j + CHUNK)
        for o in FAR_FIRST[::-1]:
            spread(j, o).wait_recv()
        hop1(j).start()
        if j + PACE < PARTS:
            send_part(j + PACE)
        if j == 0:
            forward(PARTS)
        if j >= LAG:
            forward(j - LAG)
        afull[part] = full[part].astype(F32)
    select(1)
    for j in range(PARTS - LAG, PARTS):
        forward(j)
    products(0, full, slice(0, 8))
    select(2)
    find_slots()
    for d in range(3):
        combine(d)
    v = slots_of(0)
    products(1, near1, slice(0, 8))
    v = v + slots_of(1)
    hop2(PARTS).wait_recv()
    for j in range(PARTS):
        hop2(j).wait_recv()
        products(2, near2, slice(CHUNK * j, CHUNK * j + CHUNK))
    store_slots((v + slots_of(2)) * factor)

    def core_copy(i):
        z = 1 - zh if i == 0 else zh
        return remote(vbuf.at[1 - core, z], cbuf.at[z], cs.at[i], cr.at[i], (chan, sibling))

    def slot_copy(i, dy, at, origin):
        z = 1 - zh if i == 0 else zh
        to = (y + dy) % 8
        m = 8 * i + dy
        return remote(
            vbuf.at[core, z, to], rbuf.at[at, origin], fs.at[m], fr.at[m],
            (chan, to * 4 + z * 2 + core),
        )

    for i in range(2):
        core_copy(i).start()
    for i in range(2):
        z = 1 - zh if i == 0 else zh
        core_copy(i).wait_recv()
        vbuf[core, z] += cbuf[z]
        for dy in (4, 3, 5, 2, 6, 1, 7, 0):
            if dy or i == 0:
                slot_copy(i, dy, zh, y).start()
    rbuf[zh, y] = vbuf[core, zh, y]
    for i in (1, 0):
        for dy in (1, 7, 2, 6, 3, 5, 4, 0):
            if dy or i == 0:
                slot_copy(i, dy, 1 - zh if i == 0 else zh, (y + 8 - dy) % 8).wait_recv()
    for t in range(8):
        for p in range(2):
            out_ref[p * 8 + t] = rbuf[0, t, p] + rbuf[1, t, p]

    for j in range(PARTS):
        for o in FAR_FIRST:
            spread(j, o).wait_send()
    for j in range(PARTS + 1):
        hop1(j).wait_send()
        hop2(j).wait_send()
    for i in range(2):
        core_copy(i).wait_send()
        for dy in range(8):
            if dy or i == 0:
                slot_copy(i, dy, zh, y).wait_send()


def shards(n_chan, spectra, pair_bin, bin_owner):
    channels, windows, _, freqs = spectra.shape
    factor = math.sqrt(BINS_OWN / (windows * (REACH + 1) * channels * channels))
    rows = spectra.reshape(channels, windows, 2, freqs // 128, 128)
    rows = rows.transpose(0, 1, 3, 2, 4).reshape(channels, windows, 16, 128)
    vmem = pl.BlockSpec(memory_space=pltpu.VMEM)
    dma = pltpu.SemaphoreType.DMA
    block = (8, 2, 128, 128)
    out = pl.pallas_call(
        functools.partial(kernel, n_chan, factor),
        out_shape=jax.ShapeDtypeStruct((16, 8, 128), F32),
        in_specs=[pl.BlockSpec(memory_space=pl.ANY), pl.BlockSpec(memory_space=pltpu.SMEM), vmem],
        out_specs=vmem,
        scratch_shapes=[
            pltpu.VMEM((8, 16, 16, 128), BF16),
            pltpu.VMEM((2, 256, 128), F32),
            pltpu.VMEM((8, 8, 2, 16, 128), BF16),
            pltpu.VMEM(block, BF16),
            pltpu.VMEM(block, F32),
            pltpu.VMEM(block, BF16),
            pltpu.VMEM(block, BF16),
            pltpu.VMEM((3, 2, 512, 128), F32),
            pltpu.VMEM((3, 512, 128), F32),
            pltpu.VMEM((256, 128), BF16),
            pltpu.VMEM((3, 256, 512), BF16),
            pltpu.VMEM((2, 2, 8, 2, 8, 128), F32),
            pltpu.VMEM((2, 8, 2, 8, 128), F32),
            pltpu.VMEM((2, 8, 2, 8, 128), F32),
            dma((8,)), dma((7 * PARTS,)), dma((7 * PARTS,)),
            dma((PARTS + 1,)), dma((PARTS + 1,)), dma((PARTS + 1,)), dma((PARTS + 1,)),
            dma((2,)), dma((2,)), dma((16,)), dma((16,)),
        ],
        compiler_params=pltpu.CompilerParams(
            collective_id=0, has_side_effects=True, vmem_limit_bytes=60 * 1024 * 1024
        ),
    )(rows, pair_bin.transpose(1, 0, 2), bin_owner.reshape(1, 128))
    out = out[:, :CAP].reshape(2, 8, CAP, 128).transpose(2, 0, 1, 3)
    return out.reshape(1, CAP, 2, freqs)


def solution(mesh):
    in_specs = (P("chan", "win", None, None), P("chan", None, None), P())
    out_specs = P("chan", "win", None, None)
    body = functools.partial(shards, mesh.shape["chan"])
    return jax.shard_map(body, mesh=mesh, in_specs=in_specs, out_specs=out_specs, check_vma=False)
```

time: 475 us -> 55.3 us (0.12)
  waiting for transfers between devices: 346 us -> 0 us
  Pallas kernels: 0 us -> 53.5 us
  local copies, waits for them, and re-layouts: 49.4 us -> 1.5 us
  matrix products: 35.5 us -> 0 us
  other arithmetic: 17 us -> 0 us
  between operations: 13.6 us -> 0.01 us
  starting transfers between devices: 13 us -> 0 us
    psum x1 -> x0, waiting for transfers between devices: 346 us -> none  [shards(): summed = lax.psum(stacked, 'win')]
    pallas_call x0 -> x1, Pallas kernels: none -> 53.5 us  [shards(): pl.pallas_call(functools.partial(kernel, n_chan, factor), out_shape=jax.S...]
    dot_general x6 -> x0, matrix products: 35.5 us -> none  [the longest x3 31.4 us: cross_bins(): jnp.einsum('awcf,bwcjf->abjf', near_block, partner, preferred_element_typ...]
    unnamed x12 -> x0, local copies, waits for them, and re-layouts: 23.1 us -> none
    ppermute x2 -> x0, starting transfers between devices: 13 us -> none  [shifted(): lax.ppermute(shard, axis, [(i, (i + by) % size) for i in range(size)])]
    another operation x2 -> x0, local copies, waits for them, and re-layouts: 9.53 us -> none  [cross_bins(): rotated = jnp.stack([-far_block[:, :, 1], far_block[:, :, 0]], axis=2)]
    ppermute x2 -> x0, local copies, waits for them, and re-layouts: 9.44 us -> none  [shifted(): lax.ppermute(shard, axis, [(i, (i + by) % size) for i in range(size)])]
    another operation x4 -> x0, other arithmetic: 5.75 us -> none  [the longest x2 5.64 us: cross_bins(): partner = jnp.stack([far_block, rotated], axis=3)]
  transfers between devices with their start and end apart: 3 -> 0, of which waited for: 1 -> 0; matrix products, arithmetic and copies ran while one was open for 9% -> 0% of each run, Pallas kernels for 0% -> 0%
where the time goes in v3:
time: 55.3 us; the launch traced here: 55 us
  Pallas kernels  53.5 us (97%)
  local copies, waits for them, and re-layouts  1.5 us (3%)
    pallas_call x1, Pallas kernels, shards(): pl.pallas_call(functools.partial(kernel, n_chan, factor), out_shape=jax.S...  53.5 us

profile of v3, /device:TPU:1, one launch (start us, length us, event | category | flops | bytes accessed | tf_op | source)
XLA Modules:
  0.0 55.0 jit_solution(14704031772401386425)
XLA Ops:
  0.0 53.5 %shard_map.37 = f32[16,8,128]{2,1,0:T(8,128)} custom-call(bf16[8,16,16,128]{3,2,1,0:T(8,128)(2,1)} %bitcast.13, s32[3,8,8]{2,1,0:T(8,128)} %bitcast.15, s32[1,128]{1,0:T(1,128)} %bitcast.16), custom_call_target="tpu_custom_call" | custom-call | tf_op jit(solution)/shard_map/pallas_call | solution.py:254
  53.5 0.9 %copy.5 = f32[7,2,8,128]{3,2,1,0:T(8,128)S(1)} copy(f32[7,2,8,128]{3,0,2,1:T(8,128)} %bitcast.14) | data formatting | bytes 114688 | tf_op jit(solution)/shard_map/transpose | solution.py:282
  54.3 0.7 %reshape.19 = f32[1,7,2,1024]{3,2,1,0:T(2,128)} reshape(f32[7,2,8,128]{3,2,1,0:T(8,128)S(1)} %copy.5) | data formatting | bytes 114688 | tf_op jit(solution)/shard_map/reshape | solution.py:283

commit v4 on v3

v4 whole, which is shorter than its diff:
```python
import functools
import math

import jax
import jax.numpy as jnp
from jax import lax
from jax.experimental import pallas as pl
from jax.experimental.pallas import tpu as pltpu
from jax.sharding import PartitionSpec as P

REACH = 2
BINS_OWN = 4
CAP = 7
EPS = 1e-06
F32 = jnp.float32
BF16 = jnp.bfloat16


def kernel(
    n_chan, factor,
    spec_hbm, pair_ref, owner_ref, out_ref,
    spec, tmp, wsend, line, ahead_line, near, sums, msg, rin, selt, pick, comb, vbuf, cbuf, rbuf,
    ins, ats, atr, xs, xr, ms, mr, cs, cr, fs, fr,
):
    chan = lax.axis_index("chan")
    win = lax.axis_index("win")
    x = chan // 4
    z = chan % 4
    core = win % 2
    chip = win // 2
    y = chip // 2
    zh = chip % 2
    inner = win % 4
    n_x = n_chan // 4
    x_left = (x + n_x - 1) % n_x
    x_right = (x + 1) % n_x
    sibling = win + 1 - 2 * core
    mesh_id = pl.DeviceIdType.MESH

    barrier = pltpu.get_barrier_semaphore()

    def greet(c, w):
        pl.semaphore_signal(barrier, inc=1, device_id=(c, w), device_id_type=mesh_id)

    for c in range(8):
        pltpu.make_async_copy(spec_hbm.at[c], spec.at[c], ins.at[c]).start()
    for near_x in (x_left, x_right):
        greet(near_x * 4 + z, win)
    greet(chan, sibling)
    for oy in range(8):
        for oz in range(4):
            if oy or oz:
                greet(x * 4 + (z + oz) % 4, ((y + oy) % 8) * 4 + inner)
        greet(chan, ((y + oy) % 8) * 4 + (1 - zh) * 2 + core)

    def remote(src, dst, send, recv, to):
        return pltpu.make_async_remote_copy(
            src_ref=src, dst_ref=dst, send_sem=send, recv_sem=recv, device_id=to, device_id_type=mesh_id
        )

    def spread(oy, oz, yo, zo):
        yt = (y + oy) % 8
        zt = (z + oz) % 4
        m = oy * 4 + oz
        return remote(
            wsend.at[yt, zt], line.at[zo, yo], ats.at[m], atr.at[m], (x * 4 + zt, yt * 4 + inner)
        )

    def onward(b, oy):
        yo = (y + 8 - oy) % 8
        m = b * 8 + oy
        return remote(line.at[b, yo], ahead_line.at[b, yo], xs.at[m], xr.at[m], (x_left * 4 + z, win))

    lane_block = lax.broadcasted_iota(jnp.int32, (8, 128), 1) >> 5
    top = lax.broadcasted_iota(jnp.int32, (8, 128), 0) < 4

    def whiten(cp):
        for i in range(2):
            c = 2 * cp + i
            pltpu.make_async_copy(spec_hbm.at[c], spec.at[c], ins.at[c]).wait()
            v = spec[c].astype(F32)
            power = jnp.sum(jnp.sum(v * v, axis=1, keepdims=True), axis=2, keepdims=True) * (1.0 / 2048.0)
            tmp[i] = (v * lax.rsqrt(power + EPS)).reshape(256, 128)
        for t in range(8):
            both = []
            for i in range(2):
                rl = tmp[i, pl.ds(2 * t, 8, stride=16), :]
                il = tmp[i, pl.ds(2 * t + 1, 8, stride=16), :]
                rh = tmp[i, pl.ds(128 + 2 * t, 8, stride=16), :]
                ih = tmp[i, pl.ds(129 + 2 * t, 8, stride=16), :]
                groups = [
                    jnp.where(top, rl, pltpu.roll(il, 4, 0)),
                    pltpu.roll(jnp.where(top, pltpu.roll(rl, 4, 0), il), 32, 1),
                    pltpu.roll(jnp.where(top, rh, pltpu.roll(ih, 4, 0)), 64, 1),
                    pltpu.roll(jnp.where(top, pltpu.roll(rh, 4, 0), ih), 96, 1),
                ]
                both.append(groups)
            for zt in range(4):
                halves = []
                for groups in both:
                    r = groups[3]
                    for g in range(3):
                        r = jnp.where(lane_block == (zt + g) % 4, groups[g], r)
                    halves.append(r)
                wsend[t, zt, cp] = jnp.concatenate(halves, axis=0).astype(BF16)

    for cp in range(4):
        whiten(cp)
        if cp == 0:
            pl.semaphore_wait(barrier, 42)
    for oy in (4, 3, 5, 2, 6, 1, 7, 0):
        for oz in (2, 1, 3, 0):
            if oy or oz:
                spread(oy, oz, y, z).start()
    line[z, y] = wsend[y, z]

    lanes = lax.broadcasted_iota(jnp.int32, (1, 128), 1)

    def select(d):
        def fill(j, carry):
            hit = jnp.where(lanes == pair_ref[d, j % 8, j // 8], 1.0, 0.0)
            selt[d, pl.ds(j, 1), :] = hit
            selt[d, pl.ds(j + 64, 1), :] = hit
            return carry

        lax.fori_loop(0, 64, fill, 0)

    def find_slots():
        owner = owner_ref[...].astype(F32)
        across = jnp.broadcast_to(owner, (128, 128))
        down = across.T
        rows_i = lax.broadcasted_iota(jnp.int32, (128, 128), 0)
        cols_i = lax.broadcasted_iota(jnp.int32, (128, 128), 1)
        ahead = jnp.where((across == down) & (rows_i < cols_i), 1.0, 0.0)
        slot = owner * 8.0 + jnp.sum(ahead, axis=0, keepdims=True)
        r = lax.broadcasted_iota(jnp.int32, (256, 128), 0)
        wanted = (((r >> 3) & 7) * 4 + ((r >> 6) & 1) * 2 + (r >> 7)) * 8 + (r & 7)
        pick[...] = jnp.where(wanted.astype(F32) == slot, 1.0, 0.0).astype(BF16)

    def combine(d):
        comb[d] = jnp.dot(
            pick[...], selt[d].T.astype(BF16), preferred_element_type=F32
        ).astype(BF16)

    def store_slots(v):
        for p in range(2):
            vbuf[:, :, :, p] = v[:, 128 * p:128 * p + 128].reshape(2, 2, 8, 8, 128)

    def arrive(b, oy):
        yo = (y + 8 - oy) % 8
        oz = (z + 4 - b) % 4

        def wait():
            spread(oy, oz, yo, b).wait_recv()

        if oy:
            wait()
        else:
            pl.when(z != b)(wait)
        if b < REACH:
            onward(b, oy).start()
        near[b, yo] = line[b, yo].astype(F32).reshape(8, 8, 128)

    sign = jnp.where(top, -1.0, 1.0)
    row8 = lax.broadcasted_iota(jnp.int32, (8, 128), 0)

    def halve(a, b, mask, by, axis):
        return jnp.where(mask, a, b) + pltpu.roll(jnp.where(mask, b, a), by, axis)

    def sum_rows(q):
        for by in (1, 2, 4):
            mask = (row8 & by) == 0
            q = [halve(q[2 * i], q[2 * i + 1], mask, by, 0) for i in range(len(q) // 2)]
        return q[0]

    def sum_groups(q):
        for by in (1, 2):
            mask = (lane_block & by) == 0
            q = [halve(q[2 * i], q[2 * i + 1], mask, 32 * by, 1) for i in range(len(q) // 2)]
        return q[0]

    def products(i, far, b):
        def body(kp, carry):
            re = [[None] * 8, [None] * 8]
            im = [[None] * 8, [None] * 8]
            for w in range(8):
                pair = far[b, w, kp].astype(F32)
                f = [pair[:8], pair[8:]]
                g = [pltpu.roll(q, 4, 0) * sign for q in f]
                for c in range(8):
                    a = near[i, w, c]
                    for h in range(2):
                        pr = a * f[h]
                        pi = a * g[h]
                        re[h][c] = pr if w == 0 else re[h][c] + pr
                        im[h][c] = pi if w == 0 else im[h][c] + pi
            for h in range(2):
                sums[0, h, kp] = sum_rows(re[h])
                sums[1, h, kp] = sum_rows(im[h])
            return carry

        lax.fori_loop(0, 4, body, 0)

    block16 = lax.broadcasted_iota(jnp.int32, (16, 128), 1) >> 5

    def split(rows):
        hi = rows.astype(BF16)
        return hi, (rows - hi.astype(F32)).astype(BF16)

    def fold(i, d):
        for p in range(2):
            for h in range(2):
                msg[i, d, p, 8 * h:8 * h + 8] = sum_groups([sums[p, h, g] for g in range(4)])

    def home(i, origin):
        return remote(msg.at[i], rin.at[origin], ms.at[i], mr.at[origin], (x * 4 + i, win))

    def send_home(i):
        @pl.when(z != i)
        def _():
            home(i, z).start()

    def cross(i, d):
        if i + d < 4:
            products(i, line, i + d)
        else:
            products(i, ahead_line, i + d - 4)
        fold(i, d)

    select(0)
    select(1)
    for oy in (0, 1, 7, 2, 6, 3, 5, 4):
        for b in range(2):
            arrive(b, oy)
    for oy in (0, 1, 7, 2, 6, 3, 5, 4):
        for b in range(2, 4):
            arrive(b, oy)
    for d in range(3):
        cross(0, d)
    send_home(0)
    for d in range(3):
        cross(1, d)
    send_home(1)
    cross(2, 0)
    cross(2, 1)
    cross(3, 0)
    select(2)
    find_slots()
    for d in range(3):
        combine(d)
    for oy in range(8):
        onward(0, oy).wait_recv()
    cross(3, 1)
    for oy in range(8):
        onward(1, oy).wait_recv()
    cross(3, 2)
    send_home(3)
    cross(2, 2)
    send_home(2)
    rin[z] = msg[z]
    for i in range(4):
        @pl.when(z != i)
        def _(i=i):
            home(i, i).wait_recv()

    v = None
    for d in range(3):
        parts = []
        for p in range(2):
            got = []
            for g in range(4):
                r = pltpu.roll(rin[3, d, p], 32 * ((3 - g) % 4), 1) if g != 3 else rin[3, d, p]
                for o in range(3):
                    q = rin[o, d, p]
                    if o != g:
                        q = pltpu.roll(q, 32 * ((o - g) % 4), 1)
                    r = jnp.where(block16 == o, q, r)
                got.append(r)
            parts.append(jnp.concatenate(got, axis=0))
        hi, lo = split(jnp.concatenate(parts, axis=1))
        term = jnp.dot(comb[d], jnp.concatenate([hi, lo], axis=0), preferred_element_type=F32)
        v = term if d == 0 else v + term
    store_slots(v * factor)

    def core_copy(i):
        z = 1 - zh if i == 0 else zh
        return remote(vbuf.at[1 - core, z], cbuf.at[z], cs.at[i], cr.at[i], (chan, sibling))

    def slot_copy(i, dy, at, origin):
        z = 1 - zh if i == 0 else zh
        to = (y + dy) % 8
        m = 8 * i + dy
        return remote(
            vbuf.at[core, z, to], rbuf.at[at, origin], fs.at[m], fr.at[m],
            (chan, to * 4 + z * 2 + core),
        )

    for i in range(2):
        core_copy(i).start()
    for i in range(2):
        side = 1 - zh if i == 0 else zh
        core_copy(i).wait_recv()
        vbuf[core, side] += cbuf[side]
        for dy in (4, 3, 5, 2, 6, 1, 7, 0):
            if dy or i == 0:
                slot_copy(i, dy, zh, y).start()
    rbuf[zh, y] = vbuf[core, zh, y]
    for i in (1, 0):
        for dy in (1, 7, 2, 6, 3, 5, 4, 0):
            if dy or i == 0:
                slot_copy(i, dy, 1 - zh if i == 0 else zh, (y + 8 - dy) % 8).wait_recv()
    for t in range(8):
        for p in range(2):
            out_ref[p * 8 + t] = rbuf[0, t, p] + rbuf[1, t, p]

    for oy in range(8):
        for oz in range(4):
            if oy or oz:
                spread(oy, oz, y, z).wait_send()
        for b in range(REACH):
            onward(b, oy).wait_send()
    for i in range(4):
        @pl.when(z != i)
        def _(i=i):
            home(i, z).wait_send()
    for i in range(2):
        core_copy(i).wait_send()
        for dy in range(8):
            if dy or i == 0:
                slot_copy(i, dy, zh, y).wait_send()


def shards(n_chan, spectra, pair_bin, bin_owner):
    channels, windows, _, freqs = spectra.shape
    factor = math.sqrt(BINS_OWN / (windows * (REACH + 1) * channels * channels))
    rows = spectra.reshape(channels, windows, 2, freqs // 128, 128)
    rows = rows.transpose(0, 1, 3, 2, 4).reshape(channels, windows, 16, 128)
    vmem = pl.BlockSpec(memory_space=pltpu.VMEM)
    dma = pltpu.SemaphoreType.DMA
    out = pl.pallas_call(
        functools.partial(kernel, n_chan, factor),
        out_shape=jax.ShapeDtypeStruct((16, 8, 128), F32),
        in_specs=[pl.BlockSpec(memory_space=pl.ANY), pl.BlockSpec(memory_space=pltpu.SMEM), vmem],
        out_specs=vmem,
        scratch_shapes=[
            pltpu.VMEM((8, 16, 16, 128), BF16),
            pltpu.VMEM((2, 256, 128), F32),
            pltpu.VMEM((8, 4, 4, 16, 128), BF16),
            pltpu.VMEM((4, 8, 4, 16, 128), BF16),
            pltpu.VMEM((2, 8, 4, 16, 128), BF16),
            pltpu.VMEM((4, 8, 8, 8, 128), F32),
            pltpu.VMEM((2, 2, 4, 8, 128), F32),
            pltpu.VMEM((4, 3, 2, 16, 128), F32),
            pltpu.VMEM((4, 3, 2, 16, 128), F32),
            pltpu.VMEM((3, 128, 128), F32),
            pltpu.VMEM((256, 128), BF16),
            pltpu.VMEM((3, 256, 128), BF16),
            pltpu.VMEM((2, 2, 8, 2, 8, 128), F32),
            pltpu.VMEM((2, 8, 2, 8, 128), F32),
            pltpu.VMEM((2, 8, 2, 8, 128), F32),
            dma((8,)), dma((32,)), dma((32,)), dma((16,)), dma((16,)), dma((4,)), dma((4,)),
            dma((2,)), dma((2,)), dma((16,)), dma((16,)),
        ],
        compiler_params=pltpu.CompilerParams(
            collective_id=0, has_side_effects=True, vmem_limit_bytes=60 * 1024 * 1024
        ),
    )(rows, pair_bin.transpose(1, 0, 2), bin_owner.reshape(1, 128))
    out = out[:, :CAP].reshape(2, 8, CAP, 128).transpose(2, 0, 1, 3)
    return out.reshape(1, CAP, 2, freqs)


def solution(mesh):
    in_specs = (P("chan", "win", None, None), P("chan", None, None), P())
    out_specs = P("chan", "win", None, None)
    body = functools.partial(shards, mesh.shape["chan"])
    return jax.shard_map(body, mesh=mesh, in_specs=in_specs, out_specs=out_specs, check_vma=False)
```

time: 55.3 us -> 53 us (0.958)
  the two profiles are of different devices: /device:TPU:1 before, /device:TPU:129 now
where the time goes in v4:
time: 53 us; the launch traced here: 52.8 us
  Pallas kernels  51.2 us (97%)
  local copies, waits for them, and re-layouts  1.5 us (3%)
    pallas_call x1, Pallas kernels, shards(): pl.pallas_call(functools.partial(kernel, n_chan, factor), out_shape=jax.S...  51.2 us

profile of v4, /device:TPU:129, one launch (start us, length us, event | category | flops | bytes accessed | tf_op | source)
XLA Modules:
  0.0 52.8 jit_solution(7530326209862524725)
XLA Ops:
  0.0 51.2 %shard_map.37 = f32[16,8,128]{2,1,0:T(8,128)} custom-call(bf16[8,16,16,128]{3,2,1,0:T(8,128)(2,1)} %bitcast.13, s32[3,8,8]{2,1,0:T(8,128)} %bitcast.15, s32[1,128]{1,0:T(1,128)} %bitcast.16), custom_call_target="tpu_custom_call" | custom-call | tf_op jit(solution)/shard_map/pallas_call | solution.py:340
  51.3 0.9 %copy.5 = f32[7,2,8,128]{3,2,1,0:T(8,128)S(1)} copy(f32[7,2,8,128]{3,0,2,1:T(8,128)} %bitcast.14) | data formatting | bytes 114688 | tf_op jit(solution)/shard_map/transpose | solution.py:368
  52.1 0.7 %reshape.19 = f32[1,7,2,1024]{3,2,1,0:T(2,128)} reshape(f32[7,2,8,128]{3,2,1,0:T(8,128)S(1)} %copy.5) | data formatting | bytes 114688 | tf_op jit(solution)/shard_map/reshape | solution.py:369

commit v5 on v4

--- a/solution.py
+++ b/solution.py
@@ -108,8 +108,8 @@
         whiten(cp)
         if cp == 0:
             pl.semaphore_wait(barrier, 42)
-    for oy in (4, 3, 5, 2, 6, 1, 7, 0):
-        for oz in (2, 1, 3, 0):
+    for oz in (2, 1, 3, 0):
+        for oy in (4, 3, 5, 2, 6, 1, 7, 0):
             if oy or oz:
                 spread(oy, oz, y, z).start()
     line[z, y] = wsend[y, z]
@@ -229,10 +229,14 @@
 
     select(0)
     select(1)
-    for oy in (0, 1, 7, 2, 6, 3, 5, 4):
+    select(2)
+    find_slots()
+    for d in range(3):
+        combine(d)
+    for oy in (4, 3, 5, 2, 6, 1, 7, 0):
         for b in range(2):
             arrive(b, oy)
-    for oy in (0, 1, 7, 2, 6, 3, 5, 4):
+    for oy in (4, 3, 5, 2, 6, 1, 7, 0):
         for b in range(2, 4):
             arrive(b, oy)
     for d in range(3):
@@ -244,19 +248,15 @@
     cross(2, 0)
     cross(2, 1)
     cross(3, 0)
-    select(2)
-    find_slots()
-    for d in range(3):
-        combine(d)
     for oy in range(8):
         onward(0, oy).wait_recv()
+    cross(2, 2)
+    send_home(2)
     cross(3, 1)
     for oy in range(8):
         onward(1, oy).wait_recv()
     cross(3, 2)
     send_home(3)
-    cross(2, 2)
-    send_home(2)
     rin[z] = msg[z]
     for i in range(4):
         @pl.when(z != i)

time: 53 us -> 51.6 us (0.974)
  the two profiles are of different devices: /device:TPU:129 before, /device:TPU:1 now
where the time goes in v5:
time: 51.6 us; the launch traced here: 51.4 us
  Pallas kernels  49.9 us (97%)
  local copies, waits for them, and re-layouts  1.5 us (3%)
    pallas_call x1, Pallas kernels, shards(): pl.pallas_call(functools.partial(kernel, n_chan, factor), out_shape=jax.S...  49.9 us

profile of v5, /device:TPU:1, one launch (start us, length us, event | category | flops | bytes accessed | tf_op | source)
XLA Modules:
  0.0 51.4 jit_solution(12407283479346333127)
XLA Ops:
  0.0 49.9 %shard_map.37 = f32[16,8,128]{2,1,0:T(8,128)} custom-call(bf16[8,16,16,128]{3,2,1,0:T(8,128)(2,1)} %bitcast.13, s32[3,8,8]{2,1,0:T(8,128)} %bitcast.15, s32[1,128]{1,0:T(1,128)} %bitcast.16), custom_call_target="tpu_custom_call" | custom-call | tf_op jit(solution)/shard_map/pallas_call | solution.py:340
  49.9 0.9 %copy.5 = f32[7,2,8,128]{3,2,1,0:T(8,128)S(1)} copy(f32[7,2,8,128]{3,0,2,1:T(8,128)} %bitcast.14) | data formatting | bytes 114688 | tf_op jit(solution)/shard_map/transpose | solution.py:368
  50.7 0.7 %reshape.19 = f32[1,7,2,1024]{3,2,1,0:T(2,128)} reshape(f32[7,2,8,128]{3,2,1,0:T(8,128)S(1)} %copy.5) | data formatting | bytes 114688 | tf_op jit(solution)/shard_map/reshape | solution.py:369

commit v6 on v5

--- a/solution.py
+++ b/solution.py
@@ -18,7 +18,8 @@
 
 def kernel(
     n_chan, factor,
-    spec_hbm, pair_ref, owner_ref, out_ref,
+    spec_hbm, pair_hbm, owner_hbm, out_ref,
+    pair_ref, owner_ref, small, flat,
     spec, tmp, wsend, line, ahead_line, near, sums, msg, rin, selt, pick, comb, vbuf, cbuf, rbuf,
     ins, ats, atr, xs, xr, ms, mr, cs, cr, fs, fr,
 ):
@@ -44,6 +45,10 @@
 
     for c in range(8):
         pltpu.make_async_copy(spec_hbm.at[c], spec.at[c], ins.at[c]).start()
+    pairs_in = pltpu.make_async_copy(pair_hbm, pair_ref, small.at[0])
+    owners_in = pltpu.make_async_copy(owner_hbm, owner_ref, small.at[1])
+    pairs_in.start()
+    owners_in.start()
     for near_x in (x_left, x_right):
         greet(near_x * 4 + z, win)
     greet(chan, sibling)
@@ -106,7 +111,7 @@
 
     for cp in range(4):
         whiten(cp)
-        if cp == 0:
+        if cp == 3:
             pl.semaphore_wait(barrier, 42)
     for oz in (2, 1, 3, 0):
         for oy in (4, 3, 5, 2, 6, 1, 7, 0):
@@ -121,6 +126,18 @@
             hit = jnp.where(lanes == pair_ref[d, j % 8, j // 8], 1.0, 0.0)
             selt[d, pl.ds(j, 1), :] = hit
             selt[d, pl.ds(j + 64, 1), :] = hit
+            return carry
+
+        lax.fori_loop(0, 64, fill, 0)
+
+    def select_own():
+        def fill(j, carry):
+            c, k = j % 8, j // 8
+            hit = jnp.where(lanes == pair_ref[0, c, k], 1.0, 0.0)
+            swap = jnp.where(lanes == pair_ref[0, k, c], 1.0, 0.0) * jnp.where(k > c, 1.0, 0.0)
+            for part, r in enumerate((hit + swap, hit - swap)):
+                selt[3 * part, pl.ds(j, 1), :] = r
+                selt[3 * part, pl.ds(j + 64, 1), :] = r
             return carry
 
         lax.fori_loop(0, 64, fill, 0)
@@ -181,25 +198,31 @@
 
     def products(i, far, b):
         def body(kp, carry):
-            re = [[None] * 8, [None] * 8]
-            im = [[None] * 8, [None] * 8]
+            count = [2 * kp + 1, 2 * kp + 2] if far is line and b == i else [8, 8]
+            re = [[jnp.zeros((8, 128), F32)] * 8, [jnp.zeros((8, 128), F32)] * 8]
+            im = [[jnp.zeros((8, 128), F32)] * 8, [jnp.zeros((8, 128), F32)] * 8]
             for w in range(8):
                 pair = far[b, w, kp].astype(F32)
                 f = [pair[:8], pair[8:]]
                 g = [pltpu.roll(q, 4, 0) * sign for q in f]
-                for c in range(8):
+                for c in range(count[1]):
                     a = near[i, w, c]
                     for h in range(2):
-                        pr = a * f[h]
-                        pi = a * g[h]
-                        re[h][c] = pr if w == 0 else re[h][c] + pr
-                        im[h][c] = pi if w == 0 else im[h][c] + pi
+                        if c < count[h]:
+                            pr = a * f[h]
+                            pi = a * g[h]
+                            re[h][c] = pr if w == 0 else re[h][c] + pr
+                            im[h][c] = pi if w == 0 else im[h][c] + pi
             for h in range(2):
                 sums[0, h, kp] = sum_rows(re[h])
                 sums[1, h, kp] = sum_rows(im[h])
             return carry
 
-        lax.fori_loop(0, 4, body, 0)
+        if far is line and b == i:
+            for kp in range(4):
+                body(kp, 0)
+        else:
+            lax.fori_loop(0, 4, body, 0)
 
     block16 = lax.broadcasted_iota(jnp.int32, (16, 128), 1) >> 5
 
@@ -227,11 +250,13 @@
             products(i, ahead_line, i + d - 4)
         fold(i, d)
 
-    select(0)
+    pairs_in.wait()
+    owners_in.wait()
+    select_own()
     select(1)
     select(2)
     find_slots()
-    for d in range(3):
+    for d in range(4):
         combine(d)
     for oy in (4, 3, 5, 2, 6, 1, 7, 0):
         for b in range(2):
@@ -278,7 +303,17 @@
                 got.append(r)
             parts.append(jnp.concatenate(got, axis=0))
         hi, lo = split(jnp.concatenate(parts, axis=1))
-        term = jnp.dot(comb[d], jnp.concatenate([hi, lo], axis=0), preferred_element_type=F32)
+        both = jnp.concatenate([hi, lo], axis=0)
+        if d == 0:
+            term = jnp.concatenate(
+                [
+                    jnp.dot(comb[3 * p], both[:, 128 * p:128 * p + 128], preferred_element_type=F32)
+                    for p in range(2)
+                ],
+                axis=1,
+            )
+        else:
+            term = jnp.dot(comb[d], both, preferred_element_type=F32)
         v = term if d == 0 else v + term
     store_slots(v * factor)
 
@@ -311,7 +346,8 @@
                 slot_copy(i, dy, 1 - zh if i == 0 else zh, (y + 8 - dy) % 8).wait_recv()
     for t in range(8):
         for p in range(2):
-            out_ref[p * 8 + t] = rbuf[0, t, p] + rbuf[1, t, p]
+            flat[pl.ds(2 * t + p, 8, stride=16), :] = rbuf[0, t, p] + rbuf[1, t, p]
+    out_ref[...] = flat[0:16 * CAP, :]
 
     for oy in range(8):
         for oz in range(4):
@@ -339,10 +375,14 @@
     dma = pltpu.SemaphoreType.DMA
     out = pl.pallas_call(
         functools.partial(kernel, n_chan, factor),
-        out_shape=jax.ShapeDtypeStruct((16, 8, 128), F32),
-        in_specs=[pl.BlockSpec(memory_space=pl.ANY), pl.BlockSpec(memory_space=pltpu.SMEM), vmem],
+        out_shape=jax.ShapeDtypeStruct((16 * CAP, 128), F32),
+        in_specs=[pl.BlockSpec(memory_space=pl.ANY)] * 3,
         out_specs=vmem,
         scratch_shapes=[
+            pltpu.SMEM((3, 8, 8), jnp.int32),
+            pltpu.VMEM((1, 128), jnp.int32),
+            dma((2,)),
+            pltpu.VMEM((128, 128), F32),
             pltpu.VMEM((8, 16, 16, 128), BF16),
             pltpu.VMEM((2, 256, 128), F32),
             pltpu.VMEM((8, 4, 4, 16, 128), BF16),
@@ -352,9 +392,9 @@
             pltpu.VMEM((2, 2, 4, 8, 128), F32),
             pltpu.VMEM((4, 3, 2, 16, 128), F32),
             pltpu.VMEM((4, 3, 2, 16, 128), F32),
-            pltpu.VMEM((3, 128, 128), F32),
+            pltpu.VMEM((4, 128, 128), F32),
             pltpu.VMEM((256, 128), BF16),
-            pltpu.VMEM((3, 256, 128), BF16),
+            pltpu.VMEM((4, 256, 128), BF16),
             pltpu.VMEM((2, 2, 8, 2, 8, 128), F32),
             pltpu.VMEM((2, 8, 2, 8, 128), F32),
             pltpu.VMEM((2, 8, 2, 8, 128), F32),
@@ -365,7 +405,7 @@
             collective_id=0, has_side_effects=True, vmem_limit_bytes=60 * 1024 * 1024
         ),
     )(rows, pair_bin.transpose(1, 0, 2), bin_owner.reshape(1, 128))
-    out = out[:, :CAP].reshape(2, 8, CAP, 128).transpose(2, 0, 1, 3)
+    out = out.reshape(CAP, 8, 2, 128).transpose(0, 2, 1, 3)
     return out.reshape(1, CAP, 2, freqs)
 
 

time: 51.6 us -> 49.6 us (0.961)
  Pallas kernels: 49.9 us -> 47.9 us
    pallas_call x1, Pallas kernels: 49.9 us -> 47.9 us  [shards(): pl.pallas_call(functools.partial(kernel, n_chan, factor), out_shape=jax.S...]
    unnamed x0 -> x1, local copies, waits for them, and re-layouts: none -> 1.45 us
    transpose x1 -> x0, local copies, waits for them, and re-layouts: 0.85 us -> none  [shards(): out = out[:, :CAP].reshape(2, 8, CAP, 128).transpose(2, 0, 1, 3)]
    reshape x1 -> x0, local copies, waits for them, and re-layouts: 0.65 us -> none  [shards(): return out.reshape(1, CAP, 2, freqs)]
where the time goes in v6:
time: 49.6 us; the launch traced here: 49.4 us
  Pallas kernels  47.9 us (97%)
  local copies, waits for them, and re-layouts  1.45 us (3%)
    pallas_call x1, Pallas kernels, shards(): pl.pallas_call(functools.partial(kernel, n_chan, factor), out_shape=jax.S...  47.9 us
    unnamed x1, local copies, waits for them, and re-layouts  1.45 us

profile of v6, /device:TPU:1, one launch (start us, length us, event | category | flops | bytes accessed | tf_op | source)
XLA Modules:
  0.0 49.4 jit_solution(10252505928138770749)
XLA Ops:
  0.0 47.9 %shard_map.37 = f32[112,128]{1,0:T(8,128)} custom-call(bf16[8,16,16,128]{3,2,1,0:T(8,128)(2,1)} %bitcast.12, s32[3,8,8]{2,1,0:T(8,128)} %bitcast.14, s32[1,128]{1,0:T(1,128)} %bitcast.15), custom_call_target="tpu_custom_call" | custom-call | tf_op jit(solution)/shard_map/pallas_call | solution.py:376
  47.9 1.4 %copy.7 = f32[1,7,2,1024]{3,2,1,0:T(2,128)} copy(f32[1,7,2,1024]{3,2,1,0:T(2,128)} %bitcast.13) | data formatting | bytes 114688

commit v7 on v6

--- a/solution.py
+++ b/solution.py
@@ -258,7 +258,7 @@
     find_slots()
     for d in range(4):
         combine(d)
-    for oy in (4, 3, 5, 2, 6, 1, 7, 0):
+    for oy in (1, 7, 0, 2, 6, 3, 5, 4):
         for b in range(2):
             arrive(b, oy)
     for oy in (4, 3, 5, 2, 6, 1, 7, 0):

time: 49.6 us -> 49.1 us (0.990)
  Pallas kernels: 47.9 us -> 47.4 us
where the time goes in v7:
time: 49.1 us; the launch traced here: 48.9 us
  Pallas kernels  47.4 us (97%)
  local copies, waits for them, and re-layouts  1.45 us (3%)
    pallas_call x1, Pallas kernels, shards(): pl.pallas_call(functools.partial(kernel, n_chan, factor), out_shape=jax.S...  47.4 us
    unnamed x1, local copies, waits for them, and re-layouts  1.45 us

profile of v7, /device:TPU:1, one launch (start us, length us, event | category | flops | bytes accessed | tf_op | source)
XLA Modules:
  0.0 48.9 jit_solution(10080863096709356001)
XLA Ops:
  0.0 47.4 %shard_map.37 = f32[112,128]{1,0:T(8,128)} custom-call(bf16[8,16,16,128]{3,2,1,0:T(8,128)(2,1)} %bitcast.12, s32[3,8,8]{2,1,0:T(8,128)} %bitcast.14, s32[1,128]{1,0:T(1,128)} %bitcast.15), custom_call_target="tpu_custom_call" | custom-call | tf_op jit(solution)/shard_map/pallas_call | solution.py:376
  47.4 1.4 %copy.7 = f32[1,7,2,1024]{3,2,1,0:T(2,128)} copy(f32[1,7,2,1024]{3,2,1,0:T(2,128)} %bitcast.13) | data formatting | bytes 114688

commit v8 on v7

--- a/solution.py
+++ b/solution.py
@@ -261,7 +261,7 @@
     for oy in (1, 7, 0, 2, 6, 3, 5, 4):
         for b in range(2):
             arrive(b, oy)
-    for oy in (4, 3, 5, 2, 6, 1, 7, 0):
+    for oy in (1, 7, 0, 2, 6, 3, 5, 4):
         for b in range(2, 4):
             arrive(b, oy)
     for d in range(3):

time: 49.1 us -> 49.1 us (level)
  no operation moved by 1% of the time
where the time goes in v8:
time: 49.1 us; the launch traced here: 48.9 us
  Pallas kernels  47.4 us (97%)
  local copies, waits for them, and re-layouts  1.45 us (3%)
    pallas_call x1, Pallas kernels, shards(): pl.pallas_call(functools.partial(kernel, n_chan, factor), out_shape=jax.S...  47.4 us
    unnamed x1, local copies, waits for them, and re-layouts  1.45 us

profile of v8, /device:TPU:1, one launch (start us, length us, event | category | flops | bytes accessed | tf_op | source)
XLA Modules:
  0.0 48.9 jit_solution(2369203602877742307)
XLA Ops:
  0.0 47.4 %shard_map.37 = f32[112,128]{1,0:T(8,128)} custom-call(bf16[8,16,16,128]{3,2,1,0:T(8,128)(2,1)} %bitcast.12, s32[3,8,8]{2,1,0:T(8,128)} %bitcast.14, s32[1,128]{1,0:T(1,128)} %bitcast.15), custom_call_target="tpu_custom_call" | custom-call | tf_op jit(solution)/shard_map/pallas_call | solution.py:376
  47.4 1.4 %copy.7 = f32[1,7,2,1024]{3,2,1,0:T(2,128)} copy(f32[1,7,2,1024]{3,2,1,0:T(2,128)} %bitcast.13) | data formatting | bytes 114688
